TPU v7x, 1024 devices: a whole 4x8x16 slice. The times are simulated.
1024 devices in a mesh: fsdp: 32 (over y, x), rep: 32 (over z, core).
Axes of the slice: x: 4, y: 8, z: 16, core: 2. Of those that a mesh axis runs over, the one named last changes fastest.
Arguments:
- gradient: bfloat16 [8, 128, 512, 128], P(None, 'rep', 'fsdp'), may hold values from -25 to 25
- momentum: bfloat16 [32, 64, 512, 128], P('rep', 'fsdp'), may hold values from -6 to 6
- owners: int32 [128, 8, 1], P('rep'), may hold values from 0 to 31; in each aligned block of 32 rows (0 to 31, 32 to 63, ..., all dimensions but the last counted through in order) at most 2 rows name the same one
Outputs:
- update: bfloat16 [8, 128, 512, 128], P(None, None, 'fsdp')
- momentum_new: bfloat16 [32, 64, 512, 128], P('rep', 'fsdp')
Inputs may be any that keep to these rules, and one draw needn't show every extreme that they name: `owners`: among the head blocks of one rep index (all layers), no owner is named by more than 2 blocks, and in some rep index one owner is named by exactly 2 blocks.
All inputs are finite; a program needn't handle non-finite values.
Results may differ from a plain program's by a relative error of at most 0.001.
Values may be sent and summed in bfloat16 or wider, within the bound.
A program may use at most 32 MiB of HBM per device.

v0:
```python
import math

import jax
import jax.numpy as jnp
from jax import lax
from jax.sharding import PartitionSpec as P

RANK = 512
BLOCK = 128
ITERS = 5


beta_decay = 0.95
coef_a = 3.4445
coef_b = -4.775
coef_c = 2.0315
epsilon = 1e-07


def orthogonalize(blend):
    frob_norm = jnp.sqrt(jnp.sum(blend * blend, axis=(1, 2), keepdims=True))
    current = blend / (frob_norm + epsilon)
    for step in range(ITERS):
        gram_mat = jnp.einsum("kcr,kcs->krs", current, current, precision=lax.Precision.HIGHEST)
        polynom = coef_b * gram_mat + coef_c * jnp.einsum(
            "krs,kst->krt", gram_mat, gram_mat, precision=lax.Precision.HIGHEST
        )
        current = coef_a * current + jnp.einsum(
            "kcr,krs->kcs", current, polynom, precision=lax.Precision.HIGHEST
        )
    return current


def local(gradient, momentum, owners):
    layers, blk_local, col_count, rows_head = gradient.shape
    slot_count = momentum.shape[1]
    fsdp_count = lax.axis_size("fsdp")
    flat_rows = layers * blk_local
    muon_scale = 0.2 * math.sqrt(max(RANK, BLOCK))
    owner_flat = jnp.transpose(owners[:, :, 0]).reshape(flat_rows)
    onehot_owner = (owner_flat[:, None] == jnp.arange(fsdp_count, dtype=jnp.int32)[None, :]).astype(
        jnp.int32
    )
    rank_within = jnp.cumsum(onehot_owner, axis=0) - 1
    slot_of = jnp.sum(rank_within * onehot_owner, axis=1)
    target = slot_of * fsdp_count + owner_flat
    placing = (
        target[None, :] == jnp.arange(slot_count * fsdp_count, dtype=jnp.int32)[:, None]
    ).astype(jnp.bfloat16)
    pieces = gradient.reshape(flat_rows, col_count * rows_head)
    packed = jnp.dot(placing, pieces, preferred_element_type=jnp.float32).astype(jnp.bfloat16)
    packed = packed.reshape(slot_count, fsdp_count * col_count, rows_head)
    blocks = lax.all_to_all(packed, "fsdp", split_axis=1, concat_axis=1, tiled=True)
    prior = momentum[0].astype(jnp.float32)
    fresh = blocks.astype(jnp.float32)
    carried = beta_decay * prior + fresh
    momentum_new = carried.astype(jnp.bfloat16)[None]
    blend = fresh + beta_decay * carried
    owned_update = (muon_scale * orthogonalize(blend)).astype(jnp.bfloat16)
    back_target = owner_flat * slot_count + slot_of
    unplace = (
        back_target[None, :] == jnp.arange(fsdp_count * slot_count, dtype=jnp.int32)[:, None]
    ).astype(jnp.bfloat16)
    returned = lax.all_to_all(owned_update, "fsdp", split_axis=1, concat_axis=0, tiled=True)
    unpacked = jnp.einsum(
        "qr,qcb->rcb", unplace, returned, preferred_element_type=jnp.float32
    ).astype(jnp.bfloat16)
    update = lax.all_gather(
        unpacked.reshape(layers, blk_local, col_count, returned.shape[2]), "rep", axis=1, tiled=True
    )
    return (update, momentum_new)


def solution(mesh):
    placed = (P(None, "rep", "fsdp", None), P("rep", "fsdp", None, None), P("rep", None, None))
    return jax.shard_map(
        local,
        mesh=mesh,
        in_specs=placed,
        out_specs=(P(None, None, "fsdp", None), P("rep", "fsdp", None, None)),
        check_vma=False,
    )
```

profile of v0, /device:TPU:1, one launch (start us, length us, event | category | flops | bytes accessed | tf_op | source)
XLA Modules:
  0.0 155.6 jit_solution(6737502705481455094)
XLA Ops:
  7.2 0.8 copy.21
  8.0 0.1 reshape.42
  8.1 0.1 fusion.13
  8.2 0.1 reduce_window_sum.11
  8.2 0.2 select_reduce_fusion
  8.4 1.1 convolution_convert_fusion
  9.5 0.1 reshape.44
  9.7 0.3 copy.22
  10.0 20.7 %all_to_all.23 = bf16[2,512,128]{2,0,1:T(2,128)(2,1)S(1)} all-to-all(bf16[2,512,128]{2,0,1:T(2,128)(2,1)S(1)} %copy.22), channel_id=1, replica_groups=mesh['fsdp'=32,'rep'=32] {'fsdp'}, dimensions={1} | all-to-all | bytes 524288 | tf_op jit(solution)/shard_map/all_to_all | solution.py:53
  30.7 1.8 %fusion.9 = (bf16[1,2,512,128]{3,2,1,0:T(8,128)(2,1)}, f32[2]{0:T(128)S(1)}) fusion(bf16[1,2,512,128]{3,2,1,0:T(8,128)(2,1)} %param.4, bf16[2,512,128]{2,0,1:T(2,128)(2,1)S(1)} %all_to_all.23), kind=kLoop, calls=%fused_computation.24 | loop fusion | flops 1179646 | bytes 786440 | tf_op jit(solution)/shard_map/broadcast_in_dim | solution.py:57
  32.5 2.3 %fusion.17 = f32[2,128,128]{2,1,0:T(8,128)S(1)} fusion(bf16[1,2,512,128]{3,2,1,0:T(8,128)(2,1)} %param.4, f32[2]{0:T(128)S(1)} %sqrt_add_fusion, bf16[2,512,128]{2,0,1:T(2,128)(2,1)S(1)} %all_to_all.23), kind=kOutput, calls=%fused_computation.38 | convolution fusion | flops 202244096 | bytes 655368 | tf_op jit(solution)/shard_map/kcr,kcs->krs/dot_general | solution.py:24
  34.8 0.3 fusion.6
  35.1 0.8 convolution_add_fusion.4
  35.9 1.0 fusion.20
  36.9 0.3 fusion.5
  37.2 0.6 convolution_add_fusion.3
  37.8 1.0 fusion.21
  38.8 0.3 fusion.4
  39.1 0.6 convolution_add_fusion.2
  39.7 1.0 fusion.22
  40.8 0.3 fusion.3
  41.1 0.6 convolution_add_fusion.1
  41.7 1.0 fusion.23
  42.7 0.3 fusion.2
  43.0 0.6 fusion.1
  43.6 0.3 copy.29
  43.9 13.8 %all_to_all.24 = bf16[2,512,128]{2,0,1:T(2,128)(2,1)S(1)} all-to-all(bf16[2,512,128]{2,0,1:T(2,128)(2,1)S(1)} %copy.29), channel_id=1, replica_groups=mesh['fsdp'=32,'rep'=32] {'fsdp'}, dimensions={1} | all-to-all | bytes 524288 | tf_op jit(solution)/shard_map/all_to_all | solution.py:64
  57.6 0.2 copy.30
  57.9 0.2 convolution_convert_fusion.1
  58.1 0.7 copy.31
  58.9 85.0 %all-gather.2.cloned.1.call-done = bf16[8,128,16,128]{3,2,1,0:T(8,128)(2,1)} async-done(((bf16[8,4,16,128]{3,2,1,0:T(8,128)(2,1)}), bf16[8,128,16,128]{3,2,1,0:T(8,128)(2,1)}) %all-gather.2.cloned.1.call-update) | async-done | bytes 4194320 | tf_op jit(solution)/shard_map/all_gather | solution.py:68
  143.8 4.9 %copy.51 = bf16[8,128,16,128]{3,2,1,0:T(8,128)(2,1)} copy(bf16[8,128,16,128]{3,2,1,0:T(8,128)(2,1)} %all-gather.2.cloned.1.call-done) | data formatting | bytes 8388608
  (6 shorter events, 0.1 us)
Async XLA Ops:
  7.2 27.9 %copy-start = (bf16[1,2,512,128]{3,2,1,0:T(8,128)(2,1)S(1)}, bf16[1,2,512,128]{3,2,1,0:T(8,128)(2,1)}, u32[]{:S(2)}) copy-start(bf16[1,2,512,128]{3,2,1,0:T(8,128)(2,1)} %param.4) | copy-start | bytes 786436
  7.2 136.6 %all-gather.2.cloned.1.call-start = ((), (), s32[]{:S(2)}) async-start(), calls=%async_computation.2 | async-start | bytes 4325376 | tf_op jit(solution)/shard_map/all_gather | solution.py:68
Sparse Core Ops, SparseCore 0:
  59.0 84.8 all-gather.1
where the time goes:
time: 156 us
  waiting for transfers between devices  85 us (54%)
  blocking collectives  34.5 us (22%)
  between operations  14.2 us (9%)
  matrix products  12.3 us (8%)
  local copies, waits for them, and re-layouts  7.41 us (5%)
  other arithmetic  2.16 us (1%)
    all_gather x1, waiting for transfers between devices, local(): lax.all_gather(unpacked.reshape(layers, blk_local, col_count, returned.sh...  85 us
    all_to_all x1, blocking collectives, local(): lax.all_to_all(packed, 'fsdp', split_axis=1, concat_axis=1, tiled=True)  20.7 us
    all_to_all x1, blocking collectives, local(): lax.all_to_all(owned_update, 'fsdp', split_axis=1, concat_axis=0, tiled=T...  13.8 us
    dot_general x5, matrix products, orthogonalize(): jnp.einsum('kcr,kcs->krs', current, current, precision=lax.Precision.HIGH...  6.41 us
    unnamed x3, local copies, waits for them, and re-layouts  4.93 us
    dot_general x5, matrix products, orthogonalize(): jnp.einsum('kcr,krs->kcs', current, polynom, precision=lax.Precision.HIGH...  3.23 us
  transfers between devices with their start and end apart: 1, of which 1 were waited for; matrix products, arithmetic and copies ran while one was open for 0% of the time, Pallas kernels for 0%

commit v1 on v0

--- a/solution.py
+++ b/solution.py
@@ -3,11 +3,16 @@
 import jax
 import jax.numpy as jnp
 from jax import lax
+from jax.experimental import pallas as pl
+from jax.experimental.pallas import tpu as pltpu
 from jax.sharding import PartitionSpec as P
 
 RANK = 512
 BLOCK = 128
 ITERS = 5
+CHIPS = 16
+PIECES = 4
+STEPS = 7
 
 
 beta_decay = 0.95
@@ -15,6 +20,119 @@
 coef_b = -4.775
 coef_c = 2.0315
 epsilon = 1e-07
+
+
+def gather_kernel(mine_ref, out_ref, go_sem, come_sem, give_sem, take_sem, own_sem):
+    rep = lax.axis_index("rep")
+    core = lax.rem(rep, 2)
+    chip = lax.div(rep, 2)
+    up = lax.rem(chip + 1, CHIPS) * 2 + core
+    down = lax.rem(chip + CHIPS - 1, CHIPS) * 2 + core
+    twin = chip * 2 + 1 - core
+    targets = (up, down)
+    layers, held = mine_ref.shape[:2]
+    depth = layers // PIECES
+
+    barrier = pltpu.get_barrier_semaphore()
+    for other in (up, down, twin):
+        pl.semaphore_signal(barrier, inc=1, device_id={"rep": other}, device_id_type=pl.DeviceIdType.MESH)
+    pl.semaphore_wait(barrier, 3)
+
+    def place(where, piece):
+        return out_ref.at[pl.ds(piece * depth, depth), pl.ds(where * held, held)]
+
+    def hop(way, step, piece, own):
+        if way == 0:
+            at = lax.rem(chip + CHIPS - step, CHIPS)
+        else:
+            at = lax.rem(chip + step, CHIPS)
+        dst = place(at * 2 + core, piece)
+        src = mine_ref.at[pl.ds(piece * depth, depth)] if own else dst
+        return pltpu.make_async_remote_copy(
+            src_ref=src, dst_ref=dst,
+            send_sem=go_sem.at[way, step, piece], recv_sem=come_sem.at[way, step, piece],
+            device_id={"rep": targets[way]}, device_id_type=pl.DeviceIdType.MESH)
+
+    def share(slot, at, piece, own):
+        dst = place(at * 2 + core, piece)
+        src = mine_ref.at[pl.ds(piece * depth, depth)] if own else dst
+        return pltpu.make_async_remote_copy(
+            src_ref=src, dst_ref=dst,
+            send_sem=give_sem.at[slot, piece], recv_sem=take_sem.at[slot, piece],
+            device_id={"rep": twin}, device_id_type=pl.DeviceIdType.MESH)
+
+    for piece in range(PIECES):
+        for way in range(2):
+            hop(way, 0, piece, True).start()
+    for piece in range(PIECES):
+        share(0, chip, piece, True).start()
+    own = pltpu.make_async_copy(mine_ref, out_ref.at[:, pl.ds(rep * held, held)], own_sem)
+    own.start()
+
+    def arrived(way, step, piece):
+        hop(way, step, piece, False).wait_recv()
+        if way == 0:
+            at = lax.rem(chip + CHIPS - 1 - step, CHIPS)
+        else:
+            at = lax.rem(chip + 1 + step, CHIPS)
+        return at
+
+    @pl.loop(0, STEPS - 1)
+    def _(step):
+        for piece in range(PIECES):
+            for way in range(2):
+                at = arrived(way, step, piece)
+                hop(way, step + 1, piece, False).start()
+                share(1 + 2 * step + way, at, piece, False).start()
+
+    last = STEPS - 1
+    for piece in range(PIECES):
+        for way in range(2):
+            at = arrived(way, last, piece)
+            if piece % 2 == way:
+                hop(way, last + 1, piece, False).start()
+            share(1 + 2 * last + way, at, piece, False).start()
+    for piece in range(PIECES):
+        at = arrived(piece % 2, STEPS, piece)
+        share(1 + 2 * STEPS, at, piece, False).start()
+
+    own.wait()
+
+    @pl.loop(0, STEPS)
+    def _(step):
+        for piece in range(PIECES):
+            for way in range(2):
+                hop(way, step, piece, False).wait_send()
+
+    for piece in range(PIECES):
+        hop(piece % 2, STEPS, piece, False).wait_send()
+
+    @pl.loop(0, 2 * STEPS + 2)
+    def _(slot):
+        for piece in range(PIECES):
+            both = share(slot, chip, piece, False)
+            both.wait_send()
+            both.wait_recv()
+
+
+def gather(mine):
+    layers, held, depth, width = mine.shape
+    return pl.pallas_call(
+        gather_kernel,
+        out_shape=jax.ShapeDtypeStruct((layers, held * 2 * CHIPS, depth, width), mine.dtype),
+        in_specs=[pl.BlockSpec(memory_space=pltpu.VMEM)],
+        out_specs=pl.BlockSpec(memory_space=pltpu.VMEM),
+        scratch_shapes=[
+            pltpu.SemaphoreType.DMA((2, STEPS + 1, PIECES)),
+            pltpu.SemaphoreType.DMA((2, STEPS + 1, PIECES)),
+            pltpu.SemaphoreType.DMA((2 * STEPS + 2, PIECES)),
+            pltpu.SemaphoreType.DMA((2 * STEPS + 2, PIECES)),
+            pltpu.SemaphoreType.DMA,
+        ],
+        compiler_params=pltpu.CompilerParams(
+            collective_id=1, has_side_effects=True, vmem_limit_bytes=32 * 2**20),
+        cost_estimate=pl.CostEstimate(flops=0, bytes_accessed=2**22, transcendentals=0),
+    )(mine)
 
 
 def orthogonalize(blend):
@@ -65,9 +183,7 @@
     unpacked = jnp.einsum(
         "qr,qcb->rcb", unplace, returned, preferred_element_type=jnp.float32
     ).astype(jnp.bfloat16)
-    update = lax.all_gather(
-        unpacked.reshape(layers, blk_local, col_count, returned.shape[2]), "rep", axis=1, tiled=True
-    )
+    update = gather(unpacked.reshape(layers, blk_local, col_count, returned.shape[2]))
     return (update, momentum_new)
 
 

time: 156 us -> 107 us (0.69)
  waiting for transfers between devices: 85 us -> 0 us
  Pallas kernels: 0 us -> 53.4 us
  between operations: 14.2 us -> 0.81 us
  local copies, waits for them, and re-layouts: 7.41 us -> 3.86 us
    all_gather x1 -> x0, waiting for transfers between devices: 85 us -> none  [local(): lax.all_gather(unpacked.reshape(layers, blk_local, col_count, returned.sh...]
    pallas_call x0 -> x1, Pallas kernels: none -> 53.4 us  [gather(): pl.pallas_call(gather_kernel, out_shape=jax.ShapeDtypeStruct((layers, hel...]
    unnamed x3, local copies, waits for them, and re-layouts: 4.93 us -> 2.02 us
  transfers between devices with their start and end apart: 1 -> 0, of which waited for: 1 -> 0; matrix products, arithmetic and copies ran while one was open for 0% -> 0% of each run, Pallas kernels for 0% -> 0%
where the time goes in v1:
time: 107 us
  Pallas kernels  53.4 us (50%)
  blocking collectives  34.5 us (32%)
  matrix products  12.3 us (11%)
  local copies, waits for them, and re-layouts  3.86 us (4%)
  other arithmetic  2.16 us (2%)
    pallas_call x1, Pallas kernels, gather(): pl.pallas_call(gather_kernel, out_shape=jax.ShapeDtypeStruct((layers, hel...  53.4 us
    all_to_all x1, blocking collectives, local(): lax.all_to_all(packed, 'fsdp', split_axis=1, concat_axis=1, tiled=True)  20.7 us
    all_to_all x1, blocking collectives, local(): lax.all_to_all(owned_update, 'fsdp', split_axis=1, concat_axis=0, tiled=T...  13.8 us
    dot_general x5, matrix products, orthogonalize(): jnp.einsum('kcr,kcs->krs', current, current, precision=lax.Precision.HIGH...  6.38 us
    dot_general x5, matrix products, orthogonalize(): jnp.einsum('kcr,krs->kcs', current, polynom, precision=lax.Precision.HIGH...  3.23 us

profile of v1, /device:TPU:1, one launch (start us, length us, event | category | flops | bytes accessed | tf_op | source)
XLA Modules:
  0.0 107.0 jit_solution(4281480909920120282)
XLA Ops:
  0.6 0.8 copy.21
  1.4 0.1 reshape.42
  1.5 0.1 fusion.13
  1.6 0.1 reduce_window_sum.11
  1.7 0.2 select_reduce_fusion
  1.8 1.1 %convolution_convert_fusion = bf16[64,2048]{1,0:T(8,128)(2,1)S(1)} fusion(bf16[4,8,16,128]{3,2,1,0:T(8,128)(2,1)} %bitcast.66, s32[32]{0:T(128)S(1)} %get-tuple-element.5), kind=kOutput, calls=%fused_computation | convolution fusion | flops 8521728 | bytes 393344 | tf_op jit(solution)/shard_map/dot_general | solution.py:169
  3.0 0.1 reshape.44
  3.1 0.3 copy.22
  3.4 20.7 %all_to_all.23 = bf16[2,512,128]{2,0,1:T(2,128)(2,1)S(1)} all-to-all(bf16[2,512,128]{2,0,1:T(2,128)(2,1)S(1)} %copy.22), channel_id=1, replica_groups=mesh['fsdp'=32,'rep'=32] {'fsdp'}, dimensions={1} | all-to-all | bytes 524288 | tf_op jit(solution)/shard_map/all_to_all | solution.py:171
  24.1 1.8 %fusion.9 = (bf16[1,2,512,128]{3,2,1,0:T(8,128)(2,1)}, f32[2]{0:T(128)S(1)}) fusion(bf16[1,2,512,128]{3,2,1,0:T(8,128)(2,1)} %param.4, bf16[2,512,128]{2,0,1:T(2,128)(2,1)S(1)} %all_to_all.23), kind=kLoop, calls=%fused_computation.24 | loop fusion | flops 1179646 | bytes 786440 | tf_op jit(solution)/shard_map/broadcast_in_dim | solution.py:175
  25.9 2.2 %fusion.17 = f32[2,128,128]{2,1,0:T(8,128)S(1)} fusion(bf16[1,2,512,128]{3,2,1,0:T(8,128)(2,1)} %param.4, f32[2]{0:T(128)S(1)} %sqrt_add_fusion, bf16[2,512,128]{2,0,1:T(2,128)(2,1)S(1)} %all_to_all.23), kind=kOutput, calls=%fused_computation.38 | convolution fusion | flops 202244096 | bytes 655368 | tf_op jit(solution)/shard_map/kcr,kcs->krs/dot_general | solution.py:142
  28.2 0.3 fusion.6
  28.5 0.8 convolution_add_fusion.4
  29.3 1.0 fusion.20
  30.3 0.3 fusion.5
  30.6 0.6 convolution_add_fusion.3
  31.2 1.0 fusion.21
  32.2 0.3 fusion.4
  32.5 0.6 convolution_add_fusion.2
  33.1 1.0 fusion.22
  34.2 0.3 fusion.3
  34.4 0.6 convolution_add_fusion.1
  35.1 1.0 fusion.23
  36.1 0.3 fusion.2
  36.4 0.6 fusion.1
  37.0 0.3 copy.29
  37.3 13.8 %all_to_all.24 = bf16[2,512,128]{2,0,1:T(2,128)(2,1)S(1)} all-to-all(bf16[2,512,128]{2,0,1:T(2,128)(2,1)S(1)} %copy.29), channel_id=1, replica_groups=mesh['fsdp'=32,'rep'=32] {'fsdp'}, dimensions={1} | all-to-all | bytes 524288 | tf_op jit(solution)/shard_map/all_to_all | solution.py:182
  51.0 0.2 copy.30
  51.3 0.2 convolution_convert_fusion.1
  51.5 0.1 copy.31
  51.6 53.4 %shard_map.50 = bf16[8,128,16,128]{3,2,1,0:T(8,128)(2,1)S(1)} custom-call(bf16[8,4,16,128]{3,2,1,0:T(8,128)(2,1)S(1)} %bitcast.63), custom_call_target="tpu_custom_call" | custom-call | bytes 4194304 | tf_op jit(solution)/shard_map/pallas_call | solution.py:120
  105.0 2.0 %copy.51 = bf16[8,128,16,128]{3,2,1,0:T(8,128)(2,1)} copy(bf16[8,128,16,128]{3,2,1,0:T(8,128)(2,1)S(1)} %shard_map.50) | data formatting | bytes 8388608
  (4 shorter events, 0.0 us)
Async XLA Ops:
  0.6 27.8 %copy-start = (bf16[1,2,512,128]{3,2,1,0:T(8,128)(2,1)S(1)}, bf16[1,2,512,128]{3,2,1,0:T(8,128)(2,1)}, u32[]{:S(2)}) copy-start(bf16[1,2,512,128]{3,2,1,0:T(8,128)(2,1)} %param.4) | copy-start | bytes 786436

commit v2 on v0

v2 whole, which is shorter than its diff:
```python
import functools
import math

import jax
import jax.numpy as jnp
from jax import lax
from jax.experimental import pallas as pl
from jax.experimental.pallas import tpu as pltpu
from jax.sharding import PartitionSpec as P

RANK = 512
BLOCK = 128
ROWS_Y = 8
ROWS_X = 4
CHIPS = 16
PIECES = 8
STEPS = 7
SEGMENTS = (3, 2)

beta_decay = 0.95
coef_a = 3.4445
coef_b = -4.775
coef_c = 2.0315
epsilon = 1e-07
muon_scale = 0.2 * math.sqrt(max(RANK, BLOCK))

F32 = jnp.float32
BF16 = jnp.bfloat16
MESH = pl.DeviceIdType.MESH
OFFSETS = sorted(
    [(y, x) for y in range(ROWS_Y) for x in range(ROWS_X) if (y, x) != (0, 0)],
    key=lambda o: -(min(o[0], ROWS_Y - o[0]) + min(o[1], ROWS_X - o[1])),
)


def split(value):
    high = value.astype(BF16)
    rest = value - high.astype(F32)
    mid = rest.astype(BF16)
    low = (rest - mid.astype(F32)).astype(BF16)
    return high, mid, low


def product(left, right):
    lh, lm, ll = left
    rh, rm, rl = right
    wide = jnp.concatenate([rh, rm], axis=1)
    main = jnp.dot(
        jnp.concatenate([lh, lm], axis=1), jnp.concatenate([wide, wide], axis=0), preferred_element_type=F32
    )
    rest = jnp.dot(
        jnp.concatenate([lh, ll], axis=1), jnp.concatenate([rl, rh], axis=0), preferred_element_type=F32
    )
    return main[:, :BLOCK] + (main[:, BLOCK:] + rest)


def gram(parts):
    high, mid, low = parts
    both = jnp.concatenate([high, mid], axis=1)
    dims = (((0,), (0,)), ((), ()))
    main = lax.dot_general(both, both, dims, preferred_element_type=F32)
    rest = lax.dot_general(high, low, dims, preferred_element_type=F32)
    cross = main[:BLOCK, BLOCK:] + main[BLOCK:, :BLOCK]
    return main[:BLOCK, :BLOCK] + (cross + (main[BLOCK:, BLOCK:] + (rest + rest.T)))


def orthogonalize(blends):
    row = lax.broadcasted_iota(jnp.int32, (BLOCK, BLOCK), 0)
    col = lax.broadcasted_iota(jnp.int32, (BLOCK, BLOCK), 1)
    eye = coef_a * (row == col).astype(F32)
    currents = []
    for blend in blends:
        total = jnp.sum(blend * blend, axis=(0, 1), keepdims=True)
        currents.append(blend / (jnp.sqrt(total) + epsilon))
    for count in SEGMENTS:
        parts = [split(y) for y in currents]
        grams = [gram(p) for p in parts]
        factors = None
        for step in range(count):
            pieces = [split(g) for g in grams]
            squares = [product(p, p) for p in pieces]
            polys = [split(eye + coef_b * g + coef_c * s) for g, s in zip(grams, squares)]
            if step < count - 1:
                halves = [product(p, r) for p, r in zip(pieces, polys)]
                grams = [product(split(h), r) for h, r in zip(halves, polys)]
            if factors is None:
                factors = polys
            else:
                factors = [split(product(f, r)) for f, r in zip(factors, polys)]
        currents = [product(p, f) for p, f in zip(parts, factors)]
    return currents


def kernel(
    owner_ref, gradient_ref, momentum_ref, update_ref, new_ref,
    packed, blocks, owned, returned, spread,
    out_sem, in_sem, back_sem, home_sem, self_sem,
    go_sem, come_sem, give_sem, take_sem, first_sem,
):
    rep = lax.axis_index("rep")
    me = lax.axis_index("fsdp")
    core = lax.rem(rep, 2)
    chip = lax.div(rep, 2)
    way = 1 - 2 * core
    ahead = lax.rem(chip + way + CHIPS, CHIPS) * 2 + core
    behind = lax.rem(chip - way + CHIPS, CHIPS) * 2 + core
    twin = chip * 2 + 1 - core
    mine_y = lax.div(me, ROWS_X)
    mine_x = lax.rem(me, ROWS_X)
    fsdp_count, slot_count, depth, width = packed.shape
    layers, _, _, _ = gradient_ref.shape
    held = gradient_ref.shape[1]
    flat_rows = layers * held
    block_rows = flat_rows * depth
    slot_rows = fsdp_count * slot_count * depth

    def peer(offset):
        return lax.rem(mine_y + offset[0], ROWS_Y) * ROWS_X + lax.rem(mine_x + offset[1], ROWS_X)

    barrier = pltpu.get_barrier_semaphore()
    for offset in OFFSETS:
        pl.semaphore_signal(barrier, inc=1, device_id={"fsdp": peer(offset)}, device_id_type=MESH)
    for other in (ahead, behind, twin):
        pl.semaphore_signal(barrier, inc=1, device_id={"rep": other}, device_id_type=MESH)

    names = [owner_ref[j % held, j // held] for j in range(flat_rows)]

    def targets(shape, dim):
        at = lax.broadcasted_iota(jnp.int32, shape, dim)
        number = at // depth
        owner = jnp.zeros(shape, jnp.int32)
        for j in range(flat_rows):
            owner = jnp.where(number == j, names[j], owner)
        slot = jnp.zeros(shape, jnp.int32)
        for j in range(flat_rows):
            slot += jnp.where((number > j) & (owner == names[j]), 1, 0)
        return (owner * slot_count + slot) * depth + lax.rem(at, depth)

    across = targets((1, block_rows), 1)
    place = (lax.broadcasted_iota(jnp.int32, (slot_rows, block_rows), 0) == across).astype(F32).astype(BF16)
    packed[...] = jnp.dot(
        place, gradient_ref[...].reshape(block_rows, width), preferred_element_type=F32
    ).astype(BF16).reshape(packed.shape)

    pl.semaphore_wait(barrier, len(OFFSETS) + 3)

    def swap(source, landing, sent, got, offset):
        other = peer(offset)
        return pltpu.make_async_remote_copy(
            src_ref=source.at[other], dst_ref=landing.at[me], send_sem=sent, recv_sem=got,
            device_id={"fsdp": other}, device_id_type=MESH)

    def exchange(source, landing, sent, got):
        for offset in OFFSETS:
            swap(source, landing, sent, got, offset).start()
        stays = pltpu.make_async_copy(source.at[me], landing.at[me], self_sem)
        stays.start()
        return stays

    def finish(landing, sent, got, stays):
        stays.wait()
        other = peer(OFFSETS[0])
        whole = landing.at[pl.ds(0, len(OFFSETS))]
        every = pltpu.make_async_remote_copy(
            src_ref=whole, dst_ref=whole, send_sem=sent, recv_sem=got,
            device_id={"fsdp": other}, device_id_type=MESH)
        every.wait_recv()
        every.wait_send()

    stays = exchange(packed, blocks, out_sem, in_sem)
    down = targets((block_rows, 1), 0)
    spread[...] = (lax.broadcasted_iota(jnp.int32, (block_rows, slot_rows), 1) == down).astype(F32).astype(BF16)
    finish(blocks, out_sem, in_sem, stays)

    blends = []
    for slot in range(slot_count):
        fresh = blocks[:, slot].reshape(RANK, width).astype(F32)
        carried = beta_decay * momentum_ref[0, slot].astype(F32) + fresh
        new_ref[0, slot] = carried.astype(BF16)
        blends.append(fresh + beta_decay * carried)
    for slot, current in enumerate(orthogonalize(blends)):
        owned[:, slot] = (muon_scale * current).astype(BF16).reshape(fsdp_count, depth, width)

    stays = exchange(owned, returned, back_sem, home_sem)
    finish(returned, back_sem, home_sem, stays)

    update_ref[:, pl.ds(rep * held, held)] = jnp.dot(
        spread[...], returned[...].reshape(slot_rows, width), preferred_element_type=F32
    ).astype(BF16).reshape(layers, held, depth, width)

    part = layers // PIECES

    def chunk(back, other):
        from_chip = lax.rem(chip - back * way + 2 * CHIPS, CHIPS)
        return from_chip * 2 + (core if other == 0 else 1 - core)

    def where(number, piece):
        return update_ref.at[pl.ds(piece * part, part), pl.ds(number * held, held)]

    def hop(step, other, piece):
        at = where(chunk(step, other), piece)
        return pltpu.make_async_remote_copy(
            src_ref=at, dst_ref=at, send_sem=go_sem, recv_sem=come_sem.at[step, other, piece],
            device_id={"rep": ahead}, device_id_type=MESH)

    def share(number, piece, sem):
        at = where(number, piece)
        return pltpu.make_async_remote_copy(
            src_ref=at, dst_ref=at, send_sem=give_sem, recv_sem=sem,
            device_id={"rep": twin}, device_id_type=MESH)

    for piece in range(PIECES):
        share(rep, piece, first_sem.at[piece]).start()
        hop(0, 0, piece).start()
    for piece in range(PIECES):
        share(rep, piece, first_sem.at[piece]).wait_recv()
        hop(0, 1, piece).start()

    @pl.loop(0, STEPS - 1)
    def _(step):
        for other in range(2):
            for piece in range(PIECES):
                hop(step, other, piece).wait_recv()
                hop(step + 1, other, piece).start()
                share(chunk(step + 1, other), piece, take_sem).start()

    last = STEPS - 1
    for other in range(2):
        for piece in range(PIECES):
            hop(last, other, piece).wait_recv()
            if other == 0:
                hop(STEPS, other, piece).start()
            share(chunk(STEPS, other), piece, take_sem).start()
    for piece in range(PIECES):
        hop(STEPS, 0, piece).wait_recv()
        share(chunk(STEPS + 1, 0), piece, take_sem).start()

    def chunks(number, sent, got):
        some = update_ref.at[:, pl.ds(0, number * held)]
        return pltpu.make_async_remote_copy(
            src_ref=some, dst_ref=some, send_sem=sent, recv_sem=got,
            device_id={"rep": twin}, device_id_type=MESH)

    chunks(2 * STEPS + 1, give_sem, take_sem).wait_recv()
    chunks(2 * STEPS + 1, go_sem, take_sem).wait_send()
    chunks(2 * STEPS + 2, give_sem, take_sem).wait_send()


def local(gradient, momentum, owners):
    layers, held, depth, width = gradient.shape
    slot_count = momentum.shape[1]
    fsdp_count = lax.axis_size("fsdp")
    rep_count = lax.axis_size("rep")
    vmem = pl.BlockSpec(memory_space=pltpu.VMEM)
    lanes = (fsdp_count, slot_count, depth, width)
    dma = pltpu.SemaphoreType.DMA
    update, momentum_new = pl.pallas_call(
        kernel,
        out_shape=(
            jax.ShapeDtypeStruct((layers, held * rep_count, depth, width), BF16),
            jax.ShapeDtypeStruct(momentum.shape, BF16),
        ),
        in_specs=[pl.BlockSpec(memory_space=pltpu.SMEM), vmem, vmem],
        out_specs=(vmem, vmem),
        scratch_shapes=[
            pltpu.VMEM(lanes, BF16),
            pltpu.VMEM(lanes, BF16),
            pltpu.VMEM(lanes, BF16),
            pltpu.VMEM(lanes, BF16),
            pltpu.VMEM((layers * held * depth, fsdp_count * slot_count * depth), BF16),
            dma, dma, dma, dma, dma,
            dma,
            dma((STEPS + 1, 2, PIECES)),
            dma, dma,
            dma((PIECES,)),
        ],
        compiler_params=pltpu.CompilerParams(
            collective_id=1, has_side_effects=True, vmem_limit_bytes=40 * 2**20),
        cost_estimate=pl.CostEstimate(flops=3 * 10**9, bytes_accessed=2**23, transcendentals=0),
    )(owners[:, :, 0], gradient, momentum)
    return (update, momentum_new)


def solution(mesh):
    placed = (P(None, "rep", "fsdp", None), P("rep", "fsdp", None, None), P("rep", None, None))
    return jax.shard_map(
        local,
        mesh=mesh,
        in_specs=placed,
        out_specs=(P(None, None, "fsdp", None), P("rep", "fsdp", None, None)),
        check_vma=False,
    )
```

time: 156 us -> 79.2 us (0.51)
  waiting for transfers between devices: 85 us -> 0 us
  Pallas kernels: 0 us -> 73 us
  blocking collectives: 34.5 us -> 0 us
  between operations: 14.2 us -> 0.65 us
  matrix products: 12.3 us -> 0 us
  other arithmetic: 2.16 us -> 0 us
  local copies, waits for them, and re-layouts: 7.41 us -> 5.25 us
    all_gather x1 -> x0, waiting for transfers between devices: 85 us -> none  [local(): lax.all_gather(unpacked.reshape(layers, blk_local, col_count, returned.sh...]
    pallas_call x0 -> x1, Pallas kernels: none -> 73 us  [local(): pl.pallas_call(kernel, out_shape=(jax.ShapeDtypeStruct((layers, held * re...]
    all_to_all x2 -> x0, blocking collectives: 34.5 us -> none  [the longest x1 20.7 us: local(): lax.all_to_all(packed, 'fsdp', split_axis=1, concat_axis=1, tiled=True)]
    dot_general x17 -> x0, matrix products: 12.3 us -> none  [the longest x5 6.41 us: orthogonalize(): jnp.einsum('kcr,kcs->krs', current, current, precision=lax.Precision.HIGH...]
    broadcast_in_dim x1 -> x0, other arithmetic: 1.83 us -> none  [local(): momentum_new = carried.astype(jnp.bfloat16)[None]]
    unnamed x3 -> x8, local copies, waits for them, and re-layouts: 4.93 us -> 5.25 us
  transfers between devices with their start and end apart: 1 -> 0, of which waited for: 1 -> 0; matrix products, arithmetic and copies ran while one was open for 0% -> 0% of each run, Pallas kernels for 0% -> 0%
where the time goes in v2:
time: 79.2 us; the launch traced here: 78.9 us
  Pallas kernels  73 us (92%)
  local copies, waits for them, and re-layouts  5.25 us (7%)
    pallas_call x1, Pallas kernels, local(): pl.pallas_call(kernel, out_shape=(jax.ShapeDtypeStruct((layers, held * re...  73 us
    unnamed x8, local copies, waits for them, and re-layouts  5.25 us

profile of v2, /device:TPU:1, one launch (start us, length us, event | category | flops | bytes accessed | tf_op | source)
XLA Modules:
  0.0 78.9 jit_solution(7332492562653980889)
XLA Ops:
  0.6 0.0 copy-start
  0.6 0.9 %copy-done = bf16[1,2,512,128]{3,2,1,0:T(8,128)(2,1)S(1)} copy-done((bf16[1,2,512,128]{3,2,1,0:T(8,128)(2,1)S(1)}, bf16[1,2,512,128]{3,2,1,0:T(8,128)(2,1)}, u32[]{:S(2)}) %copy-start) | copy-done | bytes 262168
  1.6 0.0 copy-start.1
  1.6 0.9 %copy-done.1 = bf16[8,4,16,128]{3,2,1,0:T(8,128)(2,1)S(1)} copy-done((bf16[8,4,16,128]{3,2,1,0:T(8,128)(2,1)S(1)}, bf16[8,4,16,128]{3,2,1,0:T(8,128)(2,1)}, u32[]{:S(2)}) %copy-start.1) | copy-done | bytes 131096
  2.5 0.0 copy-start.2
  2.5 0.7 copy-done.2
  3.2 73.0 %shard_map.50 = (bf16[8,128,16,128]{3,2,1,0:T(8,128)(2,1)S(1)}, bf16[1,2,512,128]{3,2,1,0:T(8,128)(2,1)S(1)}) custom-call(s32[4,8]{1,0:T(4,128)S(1)} %bitcast.1, bf16[8,4,16,128]{3,2,1,0:T(8,128)(2,1)S(1)} %copy-done.1, bf16[1,2,512,128]{3,2,1,0:T(8,128)(2,1)S(1)} %copy-done), custom_call_target="tpu_custom_call" | custom-call | flops 3000000000 | bytes 8388608 | tf_op jit(solution)/shard_map/pallas_call | solution.py:257
  76.2 2.0 %copy.7 = bf16[8,128,16,128]{3,2,1,0:T(8,128)(2,1)} copy(bf16[8,128,16,128]{3,2,1,0:T(8,128)(2,1)S(1)} %get-tuple-element.4) | data formatting | bytes 8388608
  78.2 0.7 copy.8
Async XLA Ops:
  0.6 1.0 %copy-start = (bf16[1,2,512,128]{3,2,1,0:T(8,128)(2,1)S(1)}, bf16[1,2,512,128]{3,2,1,0:T(8,128)(2,1)}, u32[]{:S(2)}) copy-start(bf16[1,2,512,128]{3,2,1,0:T(8,128)(2,1)} %momentum_ref.1) | copy-start | bytes 786436
  1.6 0.9 %copy-start.1 = (bf16[8,4,16,128]{3,2,1,0:T(8,128)(2,1)S(1)}, bf16[8,4,16,128]{3,2,1,0:T(8,128)(2,1)}, u32[]{:S(2)}) copy-start(bf16[8,4,16,128]{3,2,1,0:T(8,128)(2,1)} %gradient_ref.1) | copy-start | bytes 393220
  2.5 0.7 copy-start.2

commit v3 on v2

--- a/solution.py
+++ b/solution.py
@@ -14,8 +14,9 @@
 ROWS_X = 4
 CHIPS = 16
 PIECES = 8
-STEPS = 7
-SEGMENTS = (3, 2)
+ITERS = 5
+SURE = 4
+STEPS = 10
 
 beta_decay = 0.95
 coef_a = 3.4445
@@ -68,32 +69,27 @@
     row = lax.broadcasted_iota(jnp.int32, (BLOCK, BLOCK), 0)
     col = lax.broadcasted_iota(jnp.int32, (BLOCK, BLOCK), 1)
     eye = coef_a * (row == col).astype(F32)
-    currents = []
-    for blend in blends:
-        total = jnp.sum(blend * blend, axis=(0, 1), keepdims=True)
-        currents.append(blend / (jnp.sqrt(total) + epsilon))
-    for count in SEGMENTS:
+    scales = [
+        1.0 / (jnp.sqrt(jnp.sum(b * b, axis=(0, 1), keepdims=True)) + epsilon) for b in blends
+    ]
+    currents = blends
+    for step in range(ITERS):
         parts = [split(y) for y in currents]
         grams = [gram(p) for p in parts]
-        factors = None
-        for step in range(count):
-            pieces = [split(g) for g in grams]
-            squares = [product(p, p) for p in pieces]
-            polys = [split(eye + coef_b * g + coef_c * s) for g, s in zip(grams, squares)]
-            if step < count - 1:
-                halves = [product(p, r) for p, r in zip(pieces, polys)]
-                grams = [product(split(h), r) for h, r in zip(halves, polys)]
-            if factors is None:
-                factors = polys
-            else:
-                factors = [split(product(f, r)) for f, r in zip(factors, polys)]
-        currents = [product(p, f) for p, f in zip(parts, factors)]
+        if step == 0:
+            grams = [(g * v) * v for g, v in zip(grams, scales)]
+        pieces = [split(g) for g in grams]
+        squares = [product(p, p) for p in pieces]
+        factors = [eye + coef_b * g + coef_c * s for g, s in zip(grams, squares)]
+        if step == 0:
+            factors = [f * v for f, v in zip(factors, scales)]
+        currents = [product(p, split(f)) for p, f in zip(parts, factors)]
     return currents
 
 
 def kernel(
-    owner_ref, gradient_ref, momentum_ref, update_ref, new_ref,
-    packed, blocks, owned, returned, spread,
+    owner_hbm, gradient_hbm, momentum_hbm, update_ref, new_ref,
+    owner_ref, gradient_ref, momentum_ref, packed, blocks, owned, returned, spread, load_sem,
     out_sem, in_sem, back_sem, home_sem, self_sem,
     go_sem, come_sem, give_sem, take_sem, first_sem,
 ):
@@ -123,6 +119,15 @@
     for other in (ahead, behind, twin):
         pl.semaphore_signal(barrier, inc=1, device_id={"rep": other}, device_id_type=MESH)
 
+    loads = [
+        pltpu.make_async_copy(source, target, load_sem.at[i])
+        for i, (source, target) in enumerate(
+            [(owner_hbm, owner_ref), (gradient_hbm, gradient_ref), (momentum_hbm, momentum_ref)])
+    ]
+    for load in loads:
+        load.start()
+    loads[0].wait()
+
     names = [owner_ref[j % held, j // held] for j in range(flat_rows)]
 
     def targets(shape, dim):
@@ -138,6 +143,7 @@
 
     across = targets((1, block_rows), 1)
     place = (lax.broadcasted_iota(jnp.int32, (slot_rows, block_rows), 0) == across).astype(F32).astype(BF16)
+    loads[1].wait()
     packed[...] = jnp.dot(
         place, gradient_ref[...].reshape(block_rows, width), preferred_element_type=F32
     ).astype(BF16).reshape(packed.shape)
@@ -172,6 +178,7 @@
     spread[...] = (lax.broadcasted_iota(jnp.int32, (block_rows, slot_rows), 1) == down).astype(F32).astype(BF16)
     finish(blocks, out_sem, in_sem, stays)
 
+    loads[2].wait()
     blends = []
     for slot in range(slot_count):
         fresh = blocks[:, slot].reshape(RANK, width).astype(F32)
@@ -190,9 +197,21 @@
 
     part = layers // PIECES
 
+    def source(back, stream):
+        return lax.rem(chip - back * (1 - 2 * stream) + 2 * CHIPS, CHIPS)
+
+    def reach(from_chip, other, stream):
+        long = (from_chip >= 8) & (from_chip <= 10)
+        return jnp.where(long, jnp.where(stream == 1, from_chip, CHIPS - 1 - from_chip), 8 - other)
+
+    def comes(step, other, stream):
+        return step + 1 <= reach(source(step + 1, stream), other, stream)
+
+    def goes_on(step, other):
+        return step + 2 <= reach(source(step + 1, core), other, core)
+
     def chunk(back, other):
-        from_chip = lax.rem(chip - back * way + 2 * CHIPS, CHIPS)
-        return from_chip * 2 + (core if other == 0 else 1 - core)
+        return source(back, core) * 2 + (core if other == 0 else 1 - core)
 
     def where(number, piece):
         return update_ref.at[pl.ds(piece * part, part), pl.ds(number * held, held)]
@@ -200,50 +219,84 @@
     def hop(step, other, piece):
         at = where(chunk(step, other), piece)
         return pltpu.make_async_remote_copy(
-            src_ref=at, dst_ref=at, send_sem=go_sem, recv_sem=come_sem.at[step, other, piece],
+            src_ref=at, dst_ref=at, send_sem=go_sem.at[step, other], recv_sem=come_sem.at[step, other, piece],
             device_id={"rep": ahead}, device_id_type=MESH)
 
-    def share(number, piece, sem):
+    def share(number, piece, sent, got):
         at = where(number, piece)
         return pltpu.make_async_remote_copy(
-            src_ref=at, dst_ref=at, send_sem=give_sem, recv_sem=sem,
+            src_ref=at, dst_ref=at, send_sem=sent, recv_sem=got,
             device_id={"rep": twin}, device_id_type=MESH)
 
+    def pass_on(step, other, piece):
+        share(chunk(step + 1, other), piece, give_sem.at[step, other], take_sem.at[step, other]).start()
+
     for piece in range(PIECES):
-        share(rep, piece, first_sem.at[piece]).start()
+        share(rep, piece, self_sem, first_sem.at[piece]).start()
         hop(0, 0, piece).start()
     for piece in range(PIECES):
-        share(rep, piece, first_sem.at[piece]).wait_recv()
+        share(rep, piece, self_sem, first_sem.at[piece]).wait_recv()
         hop(0, 1, piece).start()
 
-    @pl.loop(0, STEPS - 1)
+    @pl.loop(0, SURE)
     def _(step):
         for other in range(2):
             for piece in range(PIECES):
                 hop(step, other, piece).wait_recv()
                 hop(step + 1, other, piece).start()
-                share(chunk(step + 1, other), piece, take_sem).start()
-
-    last = STEPS - 1
-    for other in range(2):
-        for piece in range(PIECES):
-            hop(last, other, piece).wait_recv()
-            if other == 0:
-                hop(STEPS, other, piece).start()
-            share(chunk(STEPS, other), piece, take_sem).start()
-    for piece in range(PIECES):
-        hop(STEPS, 0, piece).wait_recv()
-        share(chunk(STEPS + 1, 0), piece, take_sem).start()
-
-    def chunks(number, sent, got):
-        some = update_ref.at[:, pl.ds(0, number * held)]
+                pass_on(step, other, piece)
+
+    @pl.loop(SURE, STEPS)
+    def _(step):
+        for other in range(2):
+            @pl.when(goes_on(step, other))
+            def _():
+                for piece in range(PIECES):
+                    hop(step, other, piece).wait_recv()
+                    hop(step + 1, other, piece).start()
+                    pass_on(step, other, piece)
+
+            @pl.when(comes(step, other, core) & jnp.logical_not(goes_on(step, other)))
+            def _():
+                for piece in range(PIECES):
+                    hop(step, other, piece).wait_recv()
+                    pass_on(step, other, piece)
+
+    def whole(sent, got):
+        some = update_ref.at[:, pl.ds(rep * held, held)]
         return pltpu.make_async_remote_copy(
             src_ref=some, dst_ref=some, send_sem=sent, recv_sem=got,
             device_id={"rep": twin}, device_id_type=MESH)
 
-    chunks(2 * STEPS + 1, give_sem, take_sem).wait_recv()
-    chunks(2 * STEPS + 1, go_sem, take_sem).wait_send()
-    chunks(2 * STEPS + 2, give_sem, take_sem).wait_send()
+    whole(self_sem, self_sem).wait_send()
+    for other in range(2):
+        whole(go_sem.at[0, other], self_sem).wait_send()
+
+    @pl.loop(0, STEPS)
+    def _(step):
+        for other in range(2):
+            @pl.when(comes(step, other, core))
+            def _():
+                whole(give_sem.at[step, other], self_sem).wait_send()
+
+            @pl.when(goes_on(step, other))
+            def _():
+                whole(go_sem.at[step + 1, other], self_sem).wait_send()
+
+            @pl.when(comes(step, other, 1 - core))
+            def _():
+                whole(self_sem, take_sem.at[step, other]).wait_recv()
+
+
+def store_kernel(update_ref, new_ref, update_hbm, new_hbm, sems):
+    copies = [
+        pltpu.make_async_copy(update_ref, update_hbm, sems.at[0]),
+        pltpu.make_async_copy(new_ref, new_hbm, sems.at[1]),
+    ]
+    for copy in copies:
+        copy.start()
+    for copy in copies:
+        copy.wait()
 
 
 def local(gradient, momentum, owners):
@@ -252,6 +305,7 @@
     fsdp_count = lax.axis_size("fsdp")
     rep_count = lax.axis_size("rep")
     vmem = pl.BlockSpec(memory_space=pltpu.VMEM)
+    hbm = pl.BlockSpec(memory_space=pltpu.HBM)
     lanes = (fsdp_count, slot_count, depth, width)
     dma = pltpu.SemaphoreType.DMA
     update, momentum_new = pl.pallas_call(
@@ -260,25 +314,39 @@
             jax.ShapeDtypeStruct((layers, held * rep_count, depth, width), BF16),
             jax.ShapeDtypeStruct(momentum.shape, BF16),
         ),
-        in_specs=[pl.BlockSpec(memory_space=pltpu.SMEM), vmem, vmem],
+        in_specs=[hbm, hbm, hbm],
         out_specs=(vmem, vmem),
         scratch_shapes=[
+            pltpu.SMEM((held, layers), jnp.int32),
+            pltpu.VMEM(gradient.shape, BF16),
+            pltpu.VMEM(momentum.shape, BF16),
             pltpu.VMEM(lanes, BF16),
             pltpu.VMEM(lanes, BF16),
             pltpu.VMEM(lanes, BF16),
             pltpu.VMEM(lanes, BF16),
             pltpu.VMEM((layers * held * depth, fsdp_count * slot_count * depth), BF16),
+            dma((3,)),
             dma, dma, dma, dma, dma,
-            dma,
+            dma((STEPS + 1, 2)),
             dma((STEPS + 1, 2, PIECES)),
-            dma, dma,
+            dma((STEPS, 2)), dma((STEPS + 1, 2)),
             dma((PIECES,)),
         ],
         compiler_params=pltpu.CompilerParams(
             collective_id=1, has_side_effects=True, vmem_limit_bytes=40 * 2**20),
         cost_estimate=pl.CostEstimate(flops=3 * 10**9, bytes_accessed=2**23, transcendentals=0),
-    )(owners[:, :, 0], gradient, momentum)
-    return (update, momentum_new)
+    )(*(pltpu.with_memory_space_constraint(a, pltpu.HBM) for a in (owners[:, :, 0], gradient, momentum)))
+    return pl.pallas_call(
+        store_kernel,
+        out_shape=(
+            jax.ShapeDtypeStruct(update.shape, BF16),
+            jax.ShapeDtypeStruct(momentum_new.shape, BF16),
+        ),
+        in_specs=[vmem, vmem],
+        out_specs=(hbm, hbm),
+        scratch_shapes=[dma((2,))],
+        compiler_params=pltpu.CompilerParams(vmem_limit_bytes=16 * 2**20),
+    )(update, momentum_new)
 
 
 def solution(mesh):

time: 79.2 us -> 74.7 us (0.943)
  local copies, waits for them, and re-layouts: 5.25 us -> 0 us
  Pallas kernels: 73 us -> 73.9 us
    unnamed x8 -> x0, local copies, waits for them, and re-layouts: 5.25 us -> none
    pallas_call x0 -> x1, Pallas kernels: none -> 2.1 us  [local(): pl.pallas_call(store_kernel, out_shape=(jax.ShapeDtypeStruct(update.shape...]
    pallas_call x1, Pallas kernels: 73 us -> 71.8 us  [local(): pl.pallas_call(kernel, out_shape=(jax.ShapeDtypeStruct((layers, held * re...]
where the time goes in v3:
time: 74.7 us; the launch traced here: 74.6 us
  Pallas kernels  73.9 us (99%)
    pallas_call x1, Pallas kernels, local(): pl.pallas_call(kernel, out_shape=(jax.ShapeDtypeStruct((layers, held * re...  71.8 us
    pallas_call x1, Pallas kernels, local(): pl.pallas_call(store_kernel, out_shape=(jax.ShapeDtypeStruct(update.shape...  2.1 us

profile of v3, /device:TPU:1, one launch (start us, length us, event | category | flops | bytes accessed | tf_op | source)
XLA Modules:
  0.0 74.6 jit_solution(4638356267418671449)
XLA Ops:
  0.6 71.8 %shard_map.50 = (bf16[8,128,16,128]{3,2,1,0:T(8,128)(2,1)S(1)}, bf16[1,2,512,128]{3,2,1,0:T(8,128)(2,1)S(1)}) custom-call(s32[4,8]{1,0:T(4,128)} %bitcast.1, bf16[8,4,16,128]{3,2,1,0:T(8,128)(2,1)} %gradient_hbm.1, bf16[1,2,512,128]{3,2,1,0:T(8,128)(2,1)} %momentum_hbm.1), custom_call_target="tpu_custom_call" | custom-call | flops 3000000000 | bytes 8388608 | tf_op jit(solution)/shard_map/pallas_call | solution.py:311
  72.5 2.1 %shard_map.51 = (bf16[8,128,16,128]{3,2,1,0:T(8,128)(2,1)}, bf16[1,2,512,128]{3,2,1,0:T(8,128)(2,1)}) custom-call(bf16[8,128,16,128]{3,2,1,0:T(8,128)(2,1)S(1)} %get-tuple-element.4.update_ref, bf16[1,2,512,128]{3,2,1,0:T(8,128)(2,1)S(1)} %get-tuple-element.5.new_ref), custom_call_target="tpu_custom_call" | custom-call | tf_op jit(solution)/shard_map/pallas_call | solution.py:339

commit v4 on v3

--- a/solution.py
+++ b/solution.py
@@ -15,8 +15,7 @@
 CHIPS = 16
 PIECES = 8
 ITERS = 5
-SURE = 4
-STEPS = 10
+LAG = 6
 
 beta_decay = 0.95
 coef_a = 3.4445
@@ -32,6 +31,38 @@
     [(y, x) for y in range(ROWS_Y) for x in range(ROWS_X) if (y, x) != (0, 0)],
     key=lambda o: -(min(o[0], ROWS_Y - o[0]) + min(o[1], ROWS_X - o[1])),
 )
+
+
+DOWN = [[7, 8] for _ in range(CHIPS)]
+DOWN[8:14] = [[8, 8], [9, 9], [9, 10], [9, 9], [8, 9], [9, 9]]
+
+
+def arrivals(chip, stream):
+    items = []
+    for back in range(1, CHIPS):
+        start = (chip - back) % CHIPS if stream == 0 else (chip + back) % CHIPS
+        for other in range(2):
+            reach = DOWN[start][(stream + other) % 2]
+            if back <= (reach if stream == 1 else CHIPS - 1 - reach):
+                items.append(2 * (back - 1) + other)
+    return items
+
+
+COUNTS = [[len(arrivals(chip, stream)) for chip in range(CHIPS)] for stream in range(2)]
+ITEMS = max(map(max, COUNTS))
+for number_of in range(CHIPS):
+    for stream_of in range(2):
+        onto = COUNTS[stream_of][(number_of + 1 - 2 * stream_of) % CHIPS]
+        assert arrivals(number_of, stream_of) == list(range(COUNTS[stream_of][number_of]))
+        assert LAG <= onto - 2 <= COUNTS[stream_of][number_of]
+    assert COUNTS[0][number_of] + COUNTS[1][number_of] == 2 * (CHIPS - 1)
+
+
+def look_up(first, second, chip, core):
+    found = jnp.where(core == 0, first[0], second[0])
+    for at in range(1, CHIPS):
+        found = jnp.where(chip == at, jnp.where(core == 0, first[at], second[at]), found)
+    return found
 
 
 def split(value):
@@ -163,15 +194,15 @@
         stays.start()
         return stays
 
+    def exchanged(landing, sent, got):
+        every = landing.at[pl.ds(0, len(OFFSETS))]
+        return pltpu.make_async_remote_copy(
+            src_ref=every, dst_ref=every, send_sem=sent, recv_sem=got,
+            device_id={"fsdp": peer(OFFSETS[0])}, device_id_type=MESH)
+
     def finish(landing, sent, got, stays):
         stays.wait()
-        other = peer(OFFSETS[0])
-        whole = landing.at[pl.ds(0, len(OFFSETS))]
-        every = pltpu.make_async_remote_copy(
-            src_ref=whole, dst_ref=whole, send_sem=sent, recv_sem=got,
-            device_id={"fsdp": other}, device_id_type=MESH)
-        every.wait_recv()
-        every.wait_send()
+        exchanged(landing, sent, got).wait_recv()
 
     stays = exchange(packed, blocks, out_sem, in_sem)
     down = targets((block_rows, 1), 0)
@@ -183,12 +214,15 @@
     for slot in range(slot_count):
         fresh = blocks[:, slot].reshape(RANK, width).astype(F32)
         carried = beta_decay * momentum_ref[0, slot].astype(F32) + fresh
-        new_ref[0, slot] = carried.astype(BF16)
         blends.append(fresh + beta_decay * carried)
     for slot, current in enumerate(orthogonalize(blends)):
         owned[:, slot] = (muon_scale * current).astype(BF16).reshape(fsdp_count, depth, width)
 
     stays = exchange(owned, returned, back_sem, home_sem)
+    for slot in range(slot_count):
+        fresh = blocks[:, slot].reshape(RANK, width).astype(F32)
+        carried = beta_decay * momentum_ref[0, slot].astype(F32) + fresh
+        new_ref[0, slot] = carried.astype(BF16)
     finish(returned, back_sem, home_sem, stays)
 
     update_ref[:, pl.ds(rep * held, held)] = jnp.dot(
@@ -196,96 +230,74 @@
     ).astype(BF16).reshape(layers, held, depth, width)
 
     part = layers // PIECES
-
-    def source(back, stream):
-        return lax.rem(chip - back * (1 - 2 * stream) + 2 * CHIPS, CHIPS)
-
-    def reach(from_chip, other, stream):
-        long = (from_chip >= 8) & (from_chip <= 10)
-        return jnp.where(long, jnp.where(stream == 1, from_chip, CHIPS - 1 - from_chip), 8 - other)
-
-    def comes(step, other, stream):
-        return step + 1 <= reach(source(step + 1, stream), other, stream)
-
-    def goes_on(step, other):
-        return step + 2 <= reach(source(step + 1, core), other, core)
-
-    def chunk(back, other):
-        return source(back, core) * 2 + (core if other == 0 else 1 - core)
-
-    def where(number, piece):
-        return update_ref.at[pl.ds(piece * part, part), pl.ds(number * held, held)]
-
-    def hop(step, other, piece):
-        at = where(chunk(step, other), piece)
+    count = look_up(COUNTS[0], COUNTS[1], chip, core)
+    ahead_count = look_up(COUNTS[0][1:] + COUNTS[0][:1], COUNTS[1][-1:] + COUNTS[1][:-1], chip, core)
+    onward = ahead_count - 2
+
+    def number(item):
+        from_chip = lax.rem(chip - (lax.div(item, 2) + 1) * way + 2 * CHIPS, CHIPS)
+        return from_chip * 2 + lax.rem(core + item, 2)
+
+    def where(chunk, piece):
+        return update_ref.at[pl.ds(piece * part, part), pl.ds(chunk * held, held)]
+
+    def hop(item, at, piece):
         return pltpu.make_async_remote_copy(
-            src_ref=at, dst_ref=at, send_sem=go_sem.at[step, other], recv_sem=come_sem.at[step, other, piece],
+            src_ref=at, dst_ref=at, send_sem=go_sem.at[item], recv_sem=come_sem.at[item, piece],
             device_id={"rep": ahead}, device_id_type=MESH)
 
-    def share(number, piece, sent, got):
-        at = where(number, piece)
+    def share(at, sent, got):
         return pltpu.make_async_remote_copy(
             src_ref=at, dst_ref=at, send_sem=sent, recv_sem=got,
             device_id={"rep": twin}, device_id_type=MESH)
 
-    def pass_on(step, other, piece):
-        share(chunk(step + 1, other), piece, give_sem.at[step, other], take_sem.at[step, other]).start()
-
     for piece in range(PIECES):
-        share(rep, piece, self_sem, first_sem.at[piece]).start()
-        hop(0, 0, piece).start()
+        share(where(rep, piece), self_sem, first_sem.at[piece]).start()
+        hop(0, where(rep, piece), piece).start()
     for piece in range(PIECES):
-        share(rep, piece, self_sem, first_sem.at[piece]).wait_recv()
-        hop(0, 1, piece).start()
-
-    @pl.loop(0, SURE)
-    def _(step):
-        for other in range(2):
-            for piece in range(PIECES):
-                hop(step, other, piece).wait_recv()
-                hop(step + 1, other, piece).start()
-                pass_on(step, other, piece)
-
-    @pl.loop(SURE, STEPS)
-    def _(step):
-        for other in range(2):
-            @pl.when(goes_on(step, other))
-            def _():
-                for piece in range(PIECES):
-                    hop(step, other, piece).wait_recv()
-                    hop(step + 1, other, piece).start()
-                    pass_on(step, other, piece)
-
-            @pl.when(comes(step, other, core) & jnp.logical_not(goes_on(step, other)))
-            def _():
-                for piece in range(PIECES):
-                    hop(step, other, piece).wait_recv()
-                    pass_on(step, other, piece)
-
-    def whole(sent, got):
-        some = update_ref.at[:, pl.ds(rep * held, held)]
-        return pltpu.make_async_remote_copy(
-            src_ref=some, dst_ref=some, send_sem=sent, recv_sem=got,
-            device_id={"rep": twin}, device_id_type=MESH)
-
-    whole(self_sem, self_sem).wait_send()
-    for other in range(2):
-        whole(go_sem.at[0, other], self_sem).wait_send()
-
-    @pl.loop(0, STEPS)
-    def _(step):
-        for other in range(2):
-            @pl.when(comes(step, other, core))
-            def _():
-                whole(give_sem.at[step, other], self_sem).wait_send()
-
-            @pl.when(goes_on(step, other))
-            def _():
-                whole(go_sem.at[step + 1, other], self_sem).wait_send()
-
-            @pl.when(comes(step, other, 1 - core))
-            def _():
-                whole(self_sem, take_sem.at[step, other]).wait_recv()
+        at = where(chip * 2 + 1 - core, piece)
+        share(at, self_sem, first_sem.at[piece]).wait_recv()
+        hop(1, at, piece).start()
+
+    whole = update_ref.at[:, pl.ds(rep * held, held)]
+
+    @pl.loop(0, onward)
+    def _(item):
+        chunk = number(item)
+        for piece in range(PIECES):
+            at = where(chunk, piece)
+            hop(item, at, piece).wait_recv()
+            hop(item + 2, at, piece).start()
+            share(at, give_sem.at[item], take_sem.at[item]).start()
+
+        @pl.when(item >= LAG)
+        def _():
+            share(whole, go_sem.at[item - LAG], self_sem).wait_send()
+            share(whole, give_sem.at[item - LAG], self_sem).wait_send()
+
+    @pl.loop(onward, count)
+    def _(item):
+        chunk = number(item)
+        for piece in range(PIECES):
+            at = where(chunk, piece)
+            hop(item, at, piece).wait_recv()
+            share(at, give_sem.at[item], take_sem.at[item]).start()
+
+    share(whole, self_sem, self_sem).wait_send()
+    for sem in (out_sem, back_sem):
+        exchanged(packed, sem, sem).wait_send()
+
+    @pl.loop(onward - LAG, ahead_count)
+    def _(item):
+        share(whole, go_sem.at[item], self_sem).wait_send()
+
+    @pl.loop(onward - LAG, count)
+    def _(item):
+        share(whole, give_sem.at[item], self_sem).wait_send()
+
+    @pl.loop(0, 2 * (CHIPS - 1) - count)
+    def _(item):
+        share(whole, self_sem, take_sem.at[item]).wait_recv()
 
 
 def store_kernel(update_ref, new_ref, update_hbm, new_hbm, sems):
@@ -327,9 +339,9 @@
             pltpu.VMEM((layers * held * depth, fsdp_count * slot_count * depth), BF16),
             dma((3,)),
             dma, dma, dma, dma, dma,
-            dma((STEPS + 1, 2)),
-            dma((STEPS + 1, 2, PIECES)),
-            dma((STEPS, 2)), dma((STEPS + 1, 2)),
+            dma((ITEMS,)),
+            dma((ITEMS, PIECES)),
+            dma((ITEMS,)), dma((ITEMS,)),
             dma((PIECES,)),
         ],
         compiler_params=pltpu.CompilerParams(

time: 74.7 us -> 73.1 us (0.979)
  Pallas kernels: 73.9 us -> 72.3 us
    pallas_call x1, Pallas kernels: 71.8 us -> 70.2 us  [local(): pl.pallas_call(kernel, out_shape=(jax.ShapeDtypeStruct((layers, held * re...]
where the time goes in v4:
time: 73.1 us; the launch traced here: 72.9 us
  Pallas kernels  72.3 us (99%)
    pallas_call x1, Pallas kernels, local(): pl.pallas_call(kernel, out_shape=(jax.ShapeDtypeStruct((layers, held * re...  70.2 us
    pallas_call x1, Pallas kernels, local(): pl.pallas_call(store_kernel, out_shape=(jax.ShapeDtypeStruct(update.shape...  2.1 us

profile of v4, /device:TPU:1, one launch (start us, length us, event | category | flops | bytes accessed | tf_op | source)
XLA Modules:
  0.0 72.9 jit_solution(12424061644335976556)
XLA Ops:
  0.6 70.2 %shard_map.50 = (bf16[8,128,16,128]{3,2,1,0:T(8,128)(2,1)S(1)}, bf16[1,2,512,128]{3,2,1,0:T(8,128)(2,1)S(1)}) custom-call(s32[4,8]{1,0:T(4,128)} %bitcast.1, bf16[8,4,16,128]{3,2,1,0:T(8,128)(2,1)} %gradient_hbm.1, bf16[1,2,512,128]{3,2,1,0:T(8,128)(2,1)} %momentum_hbm.1), custom_call_target="tpu_custom_call" | custom-call | flops 3000000000 | bytes 8388608 | tf_op jit(solution)/shard_map/pallas_call | solution.py:323
  70.8 2.1 %shard_map.51 = (bf16[8,128,16,128]{3,2,1,0:T(8,128)(2,1)}, bf16[1,2,512,128]{3,2,1,0:T(8,128)(2,1)}) custom-call(bf16[8,128,16,128]{3,2,1,0:T(8,128)(2,1)S(1)} %get-tuple-element.4.update_ref, bf16[1,2,512,128]{3,2,1,0:T(8,128)(2,1)S(1)} %get-tuple-element.5.new_ref), custom_call_target="tpu_custom_call" | custom-call | tf_op jit(solution)/shard_map/pallas_call | solution.py:351

commit v5 on v4

--- a/solution.py
+++ b/solution.py
@@ -33,27 +33,25 @@
 )
 
 
-DOWN = [[7, 8] for _ in range(CHIPS)]
-DOWN[8:14] = [[8, 8], [9, 9], [9, 10], [9, 9], [8, 9], [9, 9]]
+DOWN = [7 + chip % 2 for chip in range(CHIPS)]
+DOWN[8:14] = [8, 9, 9, 9, 8, 9]
 
 
 def arrivals(chip, stream):
-    items = []
+    found = []
     for back in range(1, CHIPS):
         start = (chip - back) % CHIPS if stream == 0 else (chip + back) % CHIPS
-        for other in range(2):
-            reach = DOWN[start][(stream + other) % 2]
-            if back <= (reach if stream == 1 else CHIPS - 1 - reach):
-                items.append(2 * (back - 1) + other)
-    return items
-
-
-COUNTS = [[len(arrivals(chip, stream)) for chip in range(CHIPS)] for stream in range(2)]
+        if back <= (DOWN[start] if stream == 1 else CHIPS - 1 - DOWN[start]):
+            found.append(back)
+    return found
+
+
+COUNTS = [[2 * len(arrivals(chip, stream)) for chip in range(CHIPS)] for stream in range(2)]
 ITEMS = max(map(max, COUNTS))
 for number_of in range(CHIPS):
     for stream_of in range(2):
         onto = COUNTS[stream_of][(number_of + 1 - 2 * stream_of) % CHIPS]
-        assert arrivals(number_of, stream_of) == list(range(COUNTS[stream_of][number_of]))
+        assert arrivals(number_of, stream_of) == list(range(1, COUNTS[stream_of][number_of] // 2 + 1))
         assert LAG <= onto - 2 <= COUNTS[stream_of][number_of]
     assert COUNTS[0][number_of] + COUNTS[1][number_of] == 2 * (CHIPS - 1)
 
@@ -132,6 +130,7 @@
     ahead = lax.rem(chip + way + CHIPS, CHIPS) * 2 + core
     behind = lax.rem(chip - way + CHIPS, CHIPS) * 2 + core
     twin = chip * 2 + 1 - core
+    cross = lax.rem(chip - way + CHIPS, CHIPS) * 2 + 1 - core
     mine_y = lax.div(me, ROWS_X)
     mine_x = lax.rem(me, ROWS_X)
     fsdp_count, slot_count, depth, width = packed.shape
@@ -147,7 +146,7 @@
     barrier = pltpu.get_barrier_semaphore()
     for offset in OFFSETS:
         pl.semaphore_signal(barrier, inc=1, device_id={"fsdp": peer(offset)}, device_id_type=MESH)
-    for other in (ahead, behind, twin):
+    for other in (ahead, behind, twin, cross):
         pl.semaphore_signal(barrier, inc=1, device_id={"rep": other}, device_id_type=MESH)
 
     loads = [
@@ -179,7 +178,7 @@
         place, gradient_ref[...].reshape(block_rows, width), preferred_element_type=F32
     ).astype(BF16).reshape(packed.shape)
 
-    pl.semaphore_wait(barrier, len(OFFSETS) + 3)
+    pl.semaphore_wait(barrier, len(OFFSETS) + 4)
 
     def swap(source, landing, sent, got, offset):
         other = peer(offset)
@@ -236,7 +235,7 @@
 
     def number(item):
         from_chip = lax.rem(chip - (lax.div(item, 2) + 1) * way + 2 * CHIPS, CHIPS)
-        return from_chip * 2 + lax.rem(core + item, 2)
+        return from_chip * 2 + 1 - lax.rem(item, 2)
 
     def where(chunk, piece):
         return update_ref.at[pl.ds(piece * part, part), pl.ds(chunk * held, held)]
@@ -252,12 +251,13 @@
             device_id={"rep": twin}, device_id_type=MESH)
 
     for piece in range(PIECES):
-        share(where(rep, piece), self_sem, first_sem.at[piece]).start()
-        hop(0, where(rep, piece), piece).start()
+        at = where(rep, piece)
+        for sem, target in ((0, ahead), (1, cross)):
+            pltpu.make_async_remote_copy(
+                src_ref=at, dst_ref=at, send_sem=go_sem.at[sem], recv_sem=come_sem.at[1 - core, piece],
+                device_id={"rep": target}, device_id_type=MESH).start()
     for piece in range(PIECES):
-        at = where(chip * 2 + 1 - core, piece)
-        share(at, self_sem, first_sem.at[piece]).wait_recv()
-        hop(1, at, piece).start()
+        share(where(rep, piece), self_sem, first_sem).start()
 
     whole = update_ref.at[:, pl.ds(rep * held, held)]
 
@@ -283,7 +283,7 @@
             hop(item, at, piece).wait_recv()
             share(at, give_sem.at[item], take_sem.at[item]).start()
 
-    share(whole, self_sem, self_sem).wait_send()
+    share(whole, self_sem, first_sem).wait()
     for sem in (out_sem, back_sem):
         exchanged(packed, sem, sem).wait_send()
 
@@ -342,7 +342,7 @@
             dma((ITEMS,)),
             dma((ITEMS, PIECES)),
             dma((ITEMS,)), dma((ITEMS,)),
-            dma((PIECES,)),
+            dma,
         ],
         compiler_params=pltpu.CompilerParams(
             collective_id=1, has_side_effects=True, vmem_limit_bytes=40 * 2**20),

time: 73.1 us -> 71.3 us (0.975)
  Pallas kernels: 72.3 us -> 70.5 us
    pallas_call x1, Pallas kernels: 70.2 us -> 68.4 us  [local(): pl.pallas_call(kernel, out_shape=(jax.ShapeDtypeStruct((layers, held * re...]
where the time goes in v5:
time: 71.3 us; the launch traced here: 71.1 us
  Pallas kernels  70.5 us (99%)
    pallas_call x1, Pallas kernels, local(): pl.pallas_call(kernel, out_shape=(jax.ShapeDtypeStruct((layers, held * re...  68.4 us
    pallas_call x1, Pallas kernels, local(): pl.pallas_call(store_kernel, out_shape=(jax.ShapeDtypeStruct(update.shape...  2.1 us

profile of v5, /device:TPU:1, one launch (start us, length us, event | category | flops | bytes accessed | tf_op | source)
XLA Modules:
  0.0 71.1 jit_solution(1587173413922275369)
XLA Ops:
  0.6 68.4 %shard_map.50 = (bf16[8,128,16,128]{3,2,1,0:T(8,128)(2,1)S(1)}, bf16[1,2,512,128]{3,2,1,0:T(8,128)(2,1)S(1)}) custom-call(s32[4,8]{1,0:T(4,128)} %bitcast.1, bf16[8,4,16,128]{3,2,1,0:T(8,128)(2,1)} %gradient_hbm.1, bf16[1,2,512,128]{3,2,1,0:T(8,128)(2,1)} %momentum_hbm.1), custom_call_target="tpu_custom_call" | custom-call | flops 3000000000 | bytes 8388608 | tf_op jit(solution)/shard_map/pallas_call | solution.py:323
  69.0 2.1 %shard_map.51 = (bf16[8,128,16,128]{3,2,1,0:T(8,128)(2,1)}, bf16[1,2,512,128]{3,2,1,0:T(8,128)(2,1)}) custom-call(bf16[8,128,16,128]{3,2,1,0:T(8,128)(2,1)S(1)} %get-tuple-element.4.update_ref, bf16[1,2,512,128]{3,2,1,0:T(8,128)(2,1)S(1)} %get-tuple-element.5.new_ref), custom_call_target="tpu_custom_call" | custom-call | tf_op jit(solution)/shard_map/pallas_call | solution.py:351

commit v6 on v5

--- a/solution.py
+++ b/solution.py
@@ -222,17 +222,12 @@
         fresh = blocks[:, slot].reshape(RANK, width).astype(F32)
         carried = beta_decay * momentum_ref[0, slot].astype(F32) + fresh
         new_ref[0, slot] = carried.astype(BF16)
-    finish(returned, back_sem, home_sem, stays)
-
-    update_ref[:, pl.ds(rep * held, held)] = jnp.dot(
-        spread[...], returned[...].reshape(slot_rows, width), preferred_element_type=F32
-    ).astype(BF16).reshape(layers, held, depth, width)
-
-    part = layers // PIECES
     count = look_up(COUNTS[0], COUNTS[1], chip, core)
     ahead_count = look_up(COUNTS[0][1:] + COUNTS[0][:1], COUNTS[1][-1:] + COUNTS[1][:-1], chip, core)
     onward = ahead_count - 2
-
+    finish(returned, back_sem, home_sem, stays)
+
+    part = layers // PIECES
     def number(item):
         from_chip = lax.rem(chip - (lax.div(item, 2) + 1) * way + 2 * CHIPS, CHIPS)
         return from_chip * 2 + 1 - lax.rem(item, 2)
@@ -250,12 +245,19 @@
             src_ref=at, dst_ref=at, send_sem=sent, recv_sem=got,
             device_id={"rep": twin}, device_id_type=MESH)
 
-    for piece in range(PIECES):
-        at = where(rep, piece)
-        for sem, target in ((0, ahead), (1, cross)):
-            pltpu.make_async_remote_copy(
-                src_ref=at, dst_ref=at, send_sem=go_sem.at[sem], recv_sem=come_sem.at[1 - core, piece],
-                device_id={"rep": target}, device_id_type=MESH).start()
+    half = layers // 2
+    half_rows = block_rows // 2
+    for side in range(2):
+        update_ref[pl.ds(side * half, half), pl.ds(rep * held, held)] = jnp.dot(
+            spread[pl.ds(side * half_rows, half_rows)], returned[...].reshape(slot_rows, width),
+            preferred_element_type=F32,
+        ).astype(BF16).reshape(half, held, depth, width)
+        for piece in range(side * PIECES // 2, (side + 1) * PIECES // 2):
+            at = where(rep, piece)
+            for sem, target in ((0, ahead), (1, cross)):
+                pltpu.make_async_remote_copy(
+                    src_ref=at, dst_ref=at, send_sem=go_sem.at[sem], recv_sem=come_sem.at[1 - core, piece],
+                    device_id={"rep": target}, device_id_type=MESH).start()
     for piece in range(PIECES):
         share(where(rep, piece), self_sem, first_sem).start()
 

time: 71.3 us -> 70.9 us (level)
  no operation moved by 1% of the time
where the time goes in v6:
time: 70.9 us; the launch traced here: 70.7 us
  Pallas kernels  70.1 us (99%)
    pallas_call x1, Pallas kernels, local(): pl.pallas_call(kernel, out_shape=(jax.ShapeDtypeStruct((layers, held * re...  68 us
    pallas_call x1, Pallas kernels, local(): pl.pallas_call(store_kernel, out_shape=(jax.ShapeDtypeStruct(update.shape...  2.1 us

profile of v6, /device:TPU:1, one launch (start us, length us, event | category | flops | bytes accessed | tf_op | source)
XLA Modules:
  0.0 70.7 jit_solution(7154029521706601675)
XLA Ops:
  0.6 68.0 %shard_map.50 = (bf16[8,128,16,128]{3,2,1,0:T(8,128)(2,1)S(1)}, bf16[1,2,512,128]{3,2,1,0:T(8,128)(2,1)S(1)}) custom-call(s32[4,8]{1,0:T(4,128)} %bitcast.1, bf16[8,4,16,128]{3,2,1,0:T(8,128)(2,1)} %gradient_hbm.1, bf16[1,2,512,128]{3,2,1,0:T(8,128)(2,1)} %momentum_hbm.1), custom_call_target="tpu_custom_call" | custom-call | flops 3000000000 | bytes 8388608 | tf_op jit(solution)/shard_map/pallas_call | solution.py:325
  68.6 2.1 %shard_map.51 = (bf16[8,128,16,128]{3,2,1,0:T(8,128)(2,1)}, bf16[1,2,512,128]{3,2,1,0:T(8,128)(2,1)}) custom-call(bf16[8,128,16,128]{3,2,1,0:T(8,128)(2,1)S(1)} %get-tuple-element.4.update_ref, bf16[1,2,512,128]{3,2,1,0:T(8,128)(2,1)S(1)} %get-tuple-element.5.new_ref), custom_call_target="tpu_custom_call" | custom-call | tf_op jit(solution)/shard_map/pallas_call | solution.py:353
